TPU v7x, 128 devices: a whole 4x4x4 slice. The times are simulated.
128 devices in a mesh: leaf: 8 (over z, core), node: 16 (over y, x).
Axes of the slice: x: 4, y: 4, z: 4, core: 2. Of those that a mesh axis runs over, the one named last changes fastest.
Arguments:
- queries: bfloat16 [16384, 5120], P(('leaf', 'node')), parts along dimension 0, may hold values from -100 to 100
- leaf_kv: bfloat16 [2, 16384, 1024], P(None, ('leaf', 'node')), parts along dimension 1, may hold values from -6 to 6
- node_kv: bfloat16 [2, 128, 1024, 1024], P(None, ('leaf', 'node')), parts along dimension 1, may hold values from -6 to 6
- node_lengths: int32 [128], P('leaf'), parts along dimension 0, may hold values from 1 to 1024, 12288 in all
- ancestors: int32 [1024, 3], P(('leaf', 'node')), parts along dimension 0, may hold values from 0 to 15, all different within a row; in each aligned block of 8 rows (0 to 7, 8 to 15, ...) at most 3 rows name the same one
Outputs:
- attended: float32 [16384, 5120], P(('leaf', 'node')), parts along dimension 0
There are 8 independent parts, one for each index of `leaf`. A program takes and returns all parts, laid end to end along the dimension named above; each array names one. Nothing has to cross between parts.
Inputs may be any that keep to these rules, and one draw needn't show every extreme that they name: The 3 ancestors of a leaf are different nodes. Among the 8 leaves of one device no node is named more than 3 times, a bound that some block reaches. Node n is kept by device n // 1 of the tree. `node_lengths`: some node has all 1024 positions valid.
All inputs are finite; a program needn't handle non-finite values.
Results may differ from a plain program's by a relative error of at most 0.0026.
Values may be sent and summed in bfloat16 or wider, within the bound.
No kernel may reach another device: no remote copies, remote signals or barrier semaphores. Data moves between devices by JAX's collectives and lax.ppermute only.
A program may use at most 192 MiB of HBM per device.

v0:
```python
import functools
import jax
import jax.numpy as jnp
from jax import lax
from jax.experimental import pallas as pl
from jax.experimental.pallas import tpu as pltpu
from jax.sharding import PartitionSpec as P

SCALE2 = (128 ** -0.5) * 1.4426950408889634
LN2 = 0.6931471805599453
SPAN = 1024
R = 80
SHIFTS = (
    ((0, 0), (0, 0)),
    ((2, 0), (0, 2)),
    ((1, 1), (3, 3)),
    ((3, 1), (1, 3)),
    ((0, 1), (0, 1)),
    ((0, 3), (0, 3)),
    ((1, 0), (1, 0)),
    ((3, 0), (3, 0)),
)
COLOUR = tuple((y % 2) * 4 + (x + 2 * (y // 2)) % 4 for y in range(4) for x in range(4))
FIRST = tuple(COLOUR.index(g) for g in range(8))
SECOND = tuple(15 - COLOUR[::-1].index(g) for g in range(8))
PARTS = 2
LV = 8 // PARTS
ROWS = LV * R
LEAVES = 16 * LV
TRASH = LEAVES
CODES = 4 * LV


SIZES = (512, 768, 1024)


def pick_size(length):
    size = SIZES[-1]
    for nk in SIZES[-2::-1]:
        size = jnp.where(length <= nk, nk, size)
    return size


def iota(shape, axis):
    return lax.broadcasted_iota(jnp.int32, shape, axis)


def rank_leaves(held, tail, meta, lists, sem):
    named = tail[0].astype(jnp.float32)
    for src in range(1, 16):
        named = named + tail[src].astype(jnp.float32)
    nodes = jnp.full((128, 128), -1, jnp.int32)
    for i, node in enumerate(held):
        nodes = jnp.where(iota((128, 128), 0) == i, node, nodes)
    nodes = nodes.astype(jnp.float32)
    member = (nodes == named[0:1]) | (nodes == named[1:2]) | (nodes == named[2:3])
    member = member & (iota((128, 128), 1) < LEAVES)
    member = jnp.where(member, 1.0, 0.0).astype(jnp.bfloat16)
    lower = jnp.where(iota((128, 128), 1) <= iota((128, 128), 0), 1.0, 0.0).astype(jnp.bfloat16)
    count = lax.dot_general(lower, member, (((1,), (1,)), ((), ())), preferred_element_type=jnp.float32)
    place = iota((128, 128), 1).astype(jnp.float32)
    for i in range(len(held)):
        before = jnp.where(count[:, i:i + 1] <= place, 1.0, 0.0)
        meta[i:i + 1] = jnp.sum(before, axis=0, keepdims=True).astype(jnp.int32)
    meta[8:9] = count[127:128].astype(jnp.int32)
    copy = pltpu.make_async_copy(meta, lists, sem)
    copy.start()
    copy.wait()


def attend_kernel(slots, C, U, first, last, me_ref, lengths, q_in, *refs):
    held = len(slots)
    kv_in, refs = refs[:held], refs[held:]
    if not first:
        state_in, refs = refs[:2], refs[2:]
    if last:
        out_ref, refs = refs[0], refs[1:]
    else:
        state_out, refs = refs[:2], refs[2:]
    (kv, acc, top, tot, sa, sb, meta, lists, seen, items, lens, sem, meta_sem, state_sem, *refs) = refs
    q_ref, tail, q_sem, *refs = refs
    tail_copy = pltpu.make_async_copy(q_in.at[:, ROWS:ROWS + 16], tail, q_sem.at[0])
    tail_copy.start()
    copies = [pltpu.make_async_copy(q_in.at[:, 0:ROWS], q_ref, q_sem.at[1])]
    for i in range(held):
        for z in range(2):
            copies.append(
                pltpu.make_async_copy(kv_in[i].at[z], kv.at[i, z], sem.at[i, z])
            )
    if not first:
        for z, (a, b) in enumerate(zip(state_in, (acc, top))):
            copies.append(pltpu.make_async_copy(a, b.at[0:LEAVES], state_sem.at[z]))
    for c in copies:
        c.start()
    me = me_ref[0]
    core = me_ref[1]
    nodes = []
    for i in slots:
        dy, dx = (jnp.where(core == 0, a, b) for a, b in zip(*SHIFTS[i]))
        nodes.append((me // 4 + 4 - dy) % 4 * 4 + (me % 4 + 4 - dx) % 4)
    for i in range(held):
        lens[i] = lengths[nodes[i]]

    def clear(i, _):
        seen[i] = 0
        return 0

    lax.fori_loop(0, LEAVES + 1, clear, 0)
    tail_copy.wait()
    rank_leaves(nodes, tail, meta, lists, meta_sem)

    bounds = []
    cursor = jnp.int32(0)
    for nk in SIZES:
        start = cursor

        def node(i, cur):
            n = jnp.where(pick_size(lens[i]) == nk, lists[8, i], 0)

            def some(k, cur):
                items[0, cur] = i
                for z in range(C):
                    leaf = lists[i, jnp.minimum(C * k + z, n - 1)]
                    dest = jnp.where(C * k + z < n, leaf, TRASH)
                    items[1 + z, cur] = leaf + dest * 256 + seen[dest] * 65536
                    seen[dest] = 1
                return cur + 1

            return lax.fori_loop(0, (n + C - 1) // C, some, cur)

        cursor = lax.fori_loop(0, held, node, start)
        short = (start - cursor) % U

        def pad(k, _):
            items[0, cursor + k] = items[0, cursor - 1]
            for z in range(C):
                items[1 + z, cursor + k] = items[1 + z, cursor - 1] % 256 + TRASH * 256
            return 0

        lax.fori_loop(0, short, pad, 0)
        cursor = cursor + short
        bounds.append((start, cursor))

    for c in copies:
        c.wait()

    def scores(t, nk):
        leaves = [items[1 + z, t] % 256 for z in range(C)]
        q = jnp.concatenate(
            [q_ref[n // LV, pl.ds(pl.multiple_of(n % LV * R, 16), R)] for n in leaves], axis=0
        )
        return lax.dot_general(
            q, kv[items[0, t], 0, :nk], (((1,), (1,)), ((), ())), preferred_element_type=jnp.float32
        )

    def soften(s_ref, t, nk):
        i = items[0, t]
        sure = SIZES[SIZES.index(nk) - 1] if nk != SIZES[0] else 0
        keep = iota((1, nk - sure), 1) + sure < lens[i]
        s = jnp.where(keep, s_ref[:, sure:nk], -1e30)
        if sure:
            s = jnp.concatenate([s_ref[:, :sure], s], axis=1)
        m = jnp.max(s, axis=1, keepdims=True)
        p = jnp.exp2((s - m) * SCALE2).astype(jnp.bfloat16)
        v = jnp.concatenate([kv[i, 1, :nk], jnp.ones((nk, 128), jnp.bfloat16)], axis=1)
        o = jnp.dot(p, v, preferred_element_type=jnp.float32)
        m = jnp.broadcast_to(m * SCALE2, (C * R, 128))
        for z in range(C):
            code = items[1 + z, t]
            at = code // 256 % 256
            old = code >= 65536
            mz = m[z * R:(z + 1) * R]
            oz = o[z * R:(z + 1) * R]
            if first:
                m0 = jnp.where(old, top[at], -1e30)
                w0 = jnp.where(old, tot[at], 0.0)
                a0 = jnp.where(old, acc[at], 0.0)
            else:
                m0 = top[at]
                w0 = jnp.where(old, tot[at], 1.0)
                a0 = acc[at]
            mn = jnp.maximum(m0, mz)
            e0 = jnp.exp2(m0 - mn)
            e1 = jnp.exp2(mz - mn)
            top[at] = mn
            tot[at] = w0 * e0 + oz[:, 128:256] * e1
            acc[at] = a0 * e0 + oz[:, 0:128] * e1

    for nk, (start, end) in zip(SIZES, bounds):

        @pl.when(end > start)
        def _():
            sa[:, :nk] = scores(start, nk)

            def step(u, _):
                t = start + U * u
                for z in range(U):
                    now, then = (sa, sb) if z % 2 == 0 else (sb, sa)
                    then[:, :nk] = scores(jnp.minimum(t + z + 1, end - 1), nk)
                    soften(now, t + z, nk)
                return 0

            lax.fori_loop(0, (end - start) // U, step, 0)

    def load(n):
        old = seen[n] == 1
        if first:
            return (
                jnp.where(old, acc[n], 0.0),
                jnp.where(old, top[n], -1e30),
                jnp.where(old, tot[n], 1.0),
            )
        return acc[n], top[n], jnp.where(old, tot[n], 1.0)

    if not last:

        def even(i, _):
            for z in range(4):
                n = i * 4 + z
                a, m, w = load(n)
                acc[n] = a / w
                top[n] = m + jnp.log2(w)
            return 0

        lax.fori_loop(0, LEAVES // 4, even, 0)
        copies = [
            pltpu.make_async_copy(a.at[0:LEAVES], b, state_sem.at[z])
            for z, (a, b) in enumerate(zip((acc, top), state_out))
        ]
        for c in copies:
            c.start()
        for c in copies:
            c.wait()
        return

    out_buf, out_sem = refs
    eye = iota((R, 128), 0) == iota((R, 128), 1)

    def pick(x):
        return jnp.sum(jnp.where(eye, x, 0.0), axis=0, keepdims=True)

    def finish(dev, _):
        tops, tots = [], []
        for n in range(LV):
            a, m, w = load(dev * LV + n)
            out_buf[dev, n * R:(n + 1) * R] = (a / w).astype(jnp.bfloat16)
            tops.append(pick(m))
            tots.append(pick(w))
        used = iota((LV, 128), 1) < R
        tots = jnp.where(used, jnp.concatenate(tots, axis=0), 1.0)
        value = jnp.concatenate(tops, axis=0) * LN2 + jnp.log(tots)
        hi = value.astype(jnp.bfloat16).astype(jnp.float32)
        mid = (value - hi).astype(jnp.bfloat16).astype(jnp.float32)
        lo = value - hi - mid
        codes = jnp.concatenate([hi, mid, lo, jnp.zeros_like(lo)], axis=0)
        out_buf[dev, ROWS:ROWS + CODES] = codes.astype(jnp.bfloat16)
        pltpu.make_async_copy(out_buf.at[dev], out_ref.at[dev], out_sem.at[dev]).start()
        return 0

    lax.fori_loop(0, 16, finish, 0)
    for dev in range(16):
        pltpu.make_async_copy(out_buf.at[dev], out_ref.at[dev], out_sem.at[dev]).wait()


def attend(me, lengths, q, kvs, slots, state, last, C, U):
    smem = pl.BlockSpec(memory_space=pltpu.SMEM)
    hbm = pl.BlockSpec(memory_space=pl.ANY)
    f32 = jnp.float32
    first = state is None
    held = len(slots)
    if last:
        out_shape, out_specs = jax.ShapeDtypeStruct((16, ROWS + CODES, 128), jnp.bfloat16), hbm
    else:
        out_shape, out_specs = (jax.ShapeDtypeStruct((LEAVES, R, 128), f32),) * 2, (hbm,) * 2
    extra = () if first else state
    scratch = [
        pltpu.VMEM((held, 2, SPAN, 128), jnp.bfloat16),
        pltpu.VMEM((LEAVES + 1, R, 128), f32),
        pltpu.VMEM((LEAVES + 1, R, 128), f32),
        pltpu.VMEM((LEAVES + 1, R, 128), f32),
        pltpu.VMEM((C * R, SPAN), f32),
        pltpu.VMEM((C * R, SPAN), f32),
        pltpu.VMEM((16, 128), jnp.int32),
        pltpu.SMEM((16, 128), jnp.int32),
        pltpu.SMEM((LEAVES + 1,), jnp.int32),
        pltpu.SMEM((1 + C, 256), jnp.int32),
        pltpu.SMEM((8,), jnp.int32),
        pltpu.SemaphoreType.DMA((held, 2)),
        pltpu.SemaphoreType.DMA,
        pltpu.SemaphoreType.DMA((2,)),
        pltpu.VMEM((16, ROWS, 128), jnp.bfloat16),
        pltpu.VMEM((16, 16, 128), jnp.bfloat16),
        pltpu.SemaphoreType.DMA((2,)),
    ]
    if last:
        scratch += [pltpu.VMEM((16, ROWS + CODES, 128), jnp.bfloat16), pltpu.SemaphoreType.DMA((16,))]
    return pl.pallas_call(
        functools.partial(attend_kernel, slots, C, U, first, last),
        out_shape=out_shape,
        in_specs=[smem] * 2 + [hbm] * (1 + held + len(extra)),
        out_specs=out_specs,
        scratch_shapes=scratch,
        compiler_params=pltpu.CompilerParams(vmem_limit_bytes=62 * 1024 * 1024),
        cost_estimate=pl.CostEstimate(
            flops=held * 2_000_000_000, bytes_accessed=held * 2_000_000, transcendentals=held * 1_000_000
        ),
        name="attend" if last else "attend_near",
    )(me, lengths, q, *kvs, *extra)


def travel_pairs(i):
    pairs = []
    for tree in range(8):
        dy, dx = SHIFTS[i][tree % 2]
        for y in range(4):
            for x in range(4):
                pairs.append((tree * 16 + y * 4 + x, tree * 16 + (y + dy) % 4 * 4 + (x + dx) % 4))
    return pairs


def colour_of(y, x):
    return (y % 2) * 4 + (x + 2 * (y // 2)) % 4


def pack_queries_kernel(anc, q_ref, *refs):
    outs, (buf, sem) = refs[:PARTS], refs[PARTS:]
    me = lax.axis_index("node")
    lane = iota((16, 128), 1)
    row = iota((16, 128), 0)
    copies = []
    for part in range(PARTS):
        named = jnp.zeros((16, 128), jnp.int32)
        for n in range(LV):
            for d in range(3):
                named = jnp.where((row == d) & (lane == me * LV + n), anc[part * LV + n, d], named)
        named = named.astype(jnp.float32).astype(jnp.bfloat16)
        for g in range(8):
            for n in range(LV):
                for j in range(5):
                    at = n * R + j * 16
                    head = g * 5 + j
                    tok = (part * LV + n) * 16
                    buf[part, g, at:at + 16] = q_ref[tok:tok + 16, head * 128:(head + 1) * 128]
            buf[part, g, ROWS:ROWS + 16] = named
            for t in (FIRST[g], SECOND[g]):
                copies.append(pltpu.make_async_copy(buf.at[part, g], outs[part].at[t], sem.at[part, t]))
                copies[-1].start()
    for c in copies:
        c.wait()


def pack_queries(anc, q):
    hbm = pl.BlockSpec(memory_space=pl.ANY)
    return pl.pallas_call(
        pack_queries_kernel,
        out_shape=(jax.ShapeDtypeStruct((16, ROWS + 16, 128), jnp.bfloat16),) * PARTS,
        in_specs=[pl.BlockSpec(memory_space=pltpu.SMEM), pl.BlockSpec(memory_space=pltpu.VMEM)],
        out_specs=(hbm,) * PARTS,
        scratch_shapes=[
            pltpu.VMEM((PARTS, 8, ROWS + 16, 128), jnp.bfloat16),
            pltpu.SemaphoreType.DMA((PARTS, 16)),
        ],
        compiler_params=pltpu.CompilerParams(vmem_limit_bytes=16 * 1024 * 1024),
        name="pack_queries",
    )(anc, q)


def pack_kv_kernel(slots, kv_ref, *refs):
    outs, (buf, sem) = refs[:len(slots)], refs[len(slots):]
    me = lax.axis_index("node")
    y, x = me // 4, me % 4
    core = lax.axis_index("leaf") % 2
    loads, stores = [], []
    for n, i in enumerate(slots):
        dy, dx = (jnp.where(core == 0, a, b) for a, b in zip(*SHIFTS[i]))
        at = pl.multiple_of(colour_of((y + dy) % 4, (x + dx) % 4) * 128, 128)
        for z in range(2):
            loads.append(
                pltpu.make_async_copy(kv_ref.at[z, 0, :, pl.ds(at, 128)], buf.at[n, z], sem.at[0, n, z])
            )
            stores.append(pltpu.make_async_copy(buf.at[n, z], outs[n].at[z], sem.at[1, n, z]))
    for c in loads:
        c.start()
    for c, d in zip(loads, stores):
        c.wait()
        d.start()
    for d in stores:
        d.wait()


def pack_kv(kv, slots):
    hbm = pl.BlockSpec(memory_space=pl.ANY)
    held = len(slots)
    return pl.pallas_call(
        functools.partial(pack_kv_kernel, slots),
        out_shape=tuple(jax.ShapeDtypeStruct((2, SPAN, 128), jnp.bfloat16) for _ in slots),
        in_specs=[hbm],
        out_specs=(hbm,) * held,
        scratch_shapes=[
            pltpu.VMEM((held, 2, SPAN, 128), jnp.bfloat16),
            pltpu.SemaphoreType.DMA((2, held, 2)),
        ],
        compiler_params=pltpu.CompilerParams(vmem_limit_bytes=16 * 1024 * 1024),
        name="pack_kv",
    )(kv)


def self_kernel(q_ref, kv_ref, *refs):
    outs, lse_ref = refs[:PARTS], refs[PARTS]
    row = lax.broadcasted_iota(jnp.int32, (640, 128), 0)
    col = lax.broadcasted_iota(jnp.int32, (640, 128), 1)
    keep = (row // R == col // 16) & (col % 16 <= row % 16)
    eye = lax.broadcasted_iota(jnp.int32, (R, 128), 0) == lax.broadcasted_iota(jnp.int32, (R, 128), 1)
    for g in range(8):
        q = jnp.concatenate(
            [
                q_ref[n * 16:(n + 1) * 16, (g * 5 + j) * 128:(g * 5 + j + 1) * 128]
                for n in range(8)
                for j in range(5)
            ],
            axis=0,
        )
        k = kv_ref[0, :, g * 128:(g + 1) * 128]
        v = kv_ref[1, :, g * 128:(g + 1) * 128]
        s = lax.dot_general(q, k, (((1,), (1,)), ((), ())), preferred_element_type=jnp.float32)
        s = jnp.where(keep, s, -1e30)
        m = jnp.max(s, axis=1, keepdims=True)
        p = jnp.exp2((s - m) * SCALE2)
        l = jnp.sum(p, axis=1, keepdims=True)
        o = jnp.dot(p.astype(jnp.bfloat16), v, preferred_element_type=jnp.float32)
        o = o / l
        for part in range(PARTS):
            outs[part][g] = o[part * ROWS:(part + 1) * ROWS]
        value = jnp.broadcast_to(m * (SCALE2 * LN2) + jnp.log(l), (640, 128))
        for n in range(8):
            part = jnp.where(eye, value[n * R:(n + 1) * R], 0.0)
            lse_ref[n, g:g + 1] = jnp.sum(part, axis=0, keepdims=True)


def attend_self(q, leaf_kv):
    vmem = pl.BlockSpec(memory_space=pltpu.VMEM)
    return pl.pallas_call(
        self_kernel,
        out_shape=(jax.ShapeDtypeStruct((8, ROWS, 128), jnp.float32),) * PARTS
        + (jax.ShapeDtypeStruct((8, 8, 128), jnp.float32),),
        in_specs=[vmem] * 2,
        out_specs=(vmem,) * (PARTS + 1),
        compiler_params=pltpu.CompilerParams(vmem_limit_bytes=32 * 1024 * 1024),
        name="attend_self",
    )(q, leaf_kv)


def merge_kernel(part, back_ref, codes_ref, own_ref, own_lse, *refs):
    out_ref, lse = refs[-2:]
    leaf = pl.program_id(0)

    @pl.when(leaf == 0)
    def _():
        for g in range(8):
            for z, t in enumerate((FIRST[g], SECOND[g])):
                code = codes_ref[t].astype(jnp.float32)
                value = code[0:LV] + code[LV:2 * LV] + code[2 * LV:3 * LV]
                for n in range(LV):
                    lse[z, n, g:g + 1] = value[n:n + 1]

    l0, l1, l2 = own_lse[leaf + part * LV], lse[0, leaf], lse[1, leaf]
    top = jnp.maximum(l0, jnp.maximum(l1, l2))
    w0, w1, w2 = jnp.exp(l0 - top), jnp.exp(l1 - top), jnp.exp(l2 - top)
    inv = 1.0 / (w0 + w1 + w2)
    eye = iota((R, 128), 0) == iota((R, 128), 1)

    def spread(w, g):
        return jnp.sum(jnp.where(eye, w[g:g + 1], 0.0), axis=1, keepdims=True)

    s0, s1, s2 = w0 * inv, w1 * inv, w2 * inv
    for g in range(8):
        o = (
            spread(s0, g) * own_ref[g]
            + spread(s1, g) * back_ref[FIRST[g]].astype(jnp.float32)
            + spread(s2, g) * back_ref[SECOND[g]].astype(jnp.float32)
        )
        for j in range(5):
            out_ref[:, (g * 5 + j) * 128:(g * 5 + j + 1) * 128] = o[j * 16:(j + 1) * 16]


def merge(part, back, own, own_lse, before):
    in_specs = [
        pl.BlockSpec((16, R, 128), lambda n: (0, n, 0)),
        pl.BlockSpec((16, CODES, 128), lambda n: (0, ROWS // CODES, 0)),
        pl.BlockSpec((8, R, 128), lambda n: (0, n, 0)),
        pl.BlockSpec((8, 8, 128), lambda n: (0, 0, 0)),
    ]
    args = [back, back, own, own_lse]
    if before is not None:
        in_specs.append(pl.BlockSpec(memory_space=pl.ANY))
        args.append(before)
    return pl.pallas_call(
        functools.partial(merge_kernel, part),
        grid=(LV,),
        out_shape=jax.ShapeDtypeStruct((128, 5120), jnp.float32),
        in_specs=in_specs,
        out_specs=pl.BlockSpec((16, 5120), lambda n: (n + part * LV, 0)),
        scratch_shapes=[pltpu.VMEM((2, 8, 8, 128), jnp.float32)],
        input_output_aliases={} if before is None else {4: 0},
        compiler_params=pltpu.CompilerParams(vmem_limit_bytes=32 * 1024 * 1024),
        name="merge",
    )(*args)


NEAR = (4, 5, 6, 7)
FAR = (1, 2, 3)


def shards(queries, leaf_kv, node_kv, node_lengths, ancestors):
    me = jnp.stack([lax.axis_index("node"), lax.axis_index("leaf") % 2]).astype(jnp.int32)
    sent = list(pack_kv(node_kv, NEAR))
    loose = queries
    outgoing = list(pack_queries(ancestors, loose))
    kept, *later = pack_kv(node_kv, (0,) + FAR)

    def travel(piece, i):
        return lax.ppermute(piece, ("leaf", "node"), travel_pairs(i))

    def swap(x):
        return lax.all_to_all(x, "node", split_axis=0, concat_axis=0, tiled=True)

    arrived = [swap(outgoing[0])]
    near = [travel(piece, i) for piece, i in zip(sent, NEAR)]
    near[2], near[3], *later = lax.optimization_barrier((near[2], near[3], *later))
    near = [kept, *near]
    far = [travel(piece, i) for piece, i in zip(later, FAR)]
    held = (0,) + NEAR
    state = attend(me, node_lengths, arrived[0], near, held, None, False, 4, 2)
    done = lax.optimization_barrier((*state, *far))
    state, far = done[:2], done[2:]
    outgoing[1], *far = lax.optimization_barrier((outgoing[1], *far))
    arrived.append(swap(outgoing[1]))
    answer = attend(me, node_lengths, arrived[0], far, FAR, state, True, 4, 2)
    *own, own_lse = attend_self(queries, leaf_kv)
    out = merge(0, swap(answer), own[0], own_lse, None)
    answer = attend(me, node_lengths, arrived[1], near + far, held + FAR, None, True, 4, 2)
    return merge(1, swap(answer), own[1], own_lse, out)


def solution(mesh):
    placed = (
        P(("leaf", "node"), None),
        P(None, ("leaf", "node"), None),
        P(None, ("leaf", "node"), None, None),
        P("leaf"),
        P(("leaf", "node"), None),
    )
    return jax.shard_map(
        shards, mesh=mesh, in_specs=placed, out_specs=P(("leaf", "node"), None), check_vma=False
    )
```

profile of v0, /device:TPU:96, one launch (start us, length us, event | category | flops | bytes accessed | tf_op | source)
XLA Modules:
  0.0 154.9 jit_solution(17569764976509453719)
XLA Ops:
  0.0 0.8 copy.7.anc
  0.8 1.3 copy-done.2
  2.1 2.4 %pack_queries.1 = (bf16[16,336,128]{2,1,0:T(8,128)(2,1)}, bf16[16,336,128]{2,1,0:T(8,128)(2,1)}) custom-call(s32[8,3]{1,0:T(8,128)S(1)} %copy.7.anc, bf16[128,5120]{1,0:T(8,128)(2,1)S(1)} %copy-done.2), custom_call_target="tpu_custom_call" | custom-call | tf_op jit(solution)/shard_map/pack_queries/pallas_call | solution.py:354
  4.5 7.1 %all-to-all-start = ((bf16[16,336,128]{2,1,0:T(8,128)(2,1)}), bf16[16,336,128]{2,1,0:T(8,128)(2,1)}, u32[]{:S(2)}, u32[]{:S(2)}) async-start(bf16[16,336,128]{2,1,0:T(8,128)(2,1)} %get-tuple-element.35), calls=%async_computation | async-start | bytes 2752512 | tf_op jit(solution)/shard_map/all_to_all | solution.py:525
  11.6 0.0 copy-start
  11.6 2.2 %copy-done = bf16[2,1,1024,1024]{3,2,1,0:T(8,128)(2,1)S(1)} copy-done((bf16[2,1,1024,1024]{3,2,1,0:T(8,128)(2,1)S(1)}, bf16[2,1,1024,1024]{3,2,1,0:T(8,128)(2,1)}, u32[]{:S(2)}) %copy-start) | copy-done | bytes 4194328
  13.8 0.9 pack_kv.3
  14.6 1.9 %collective-permute-start.2 = (bf16[2,1024,128]{2,1,0:T(8,128)(2,1)S(1)}, bf16[2,1024,128]{2,1,0:T(8,128)(2,1)}, u32[]{:S(2)}, u32[]{:S(2)}) collective-permute-start(bf16[2,1024,128]{2,1,0:T(8,128)(2,1)S(1)} %get-tuple-element.39), channel_id=1, source_target_pairs={{0,4},{1,5},{2,6},{3,7},{4,8},{5,9},{6,10},{7,11},{8,12},{9,13},{1... | collective-permute-start | bytes 1572872 | tf_op jit(solution)/shard_map/ppermute | solution.py:522
  16.6 1.4 collective-permute-start.3
  17.9 1.9 %collective-permute-start = (bf16[2,1024,128]{2,1,0:T(8,128)(2,1)S(1)}, bf16[2,1024,128]{2,1,0:T(8,128)(2,1)}, u32[]{:S(2)}, u32[]{:S(2)}) collective-permute-start(bf16[2,1024,128]{2,1,0:T(8,128)(2,1)S(1)} %get-tuple-element.37), channel_id=1, source_target_pairs={{0,1},{1,2},{2,3},{3,0},{4,5},{5,6},{6,7},{7,4},{8,9},{9,10},{10,1... | collective-permute-start | bytes 1572872 | tf_op jit(solution)/shard_map/ppermute | solution.py:522
  19.8 1.4 collective-permute-start.1
  21.2 2.2 %copy-done.1 = bf16[2,1,1024,1024]{3,2,1,0:T(8,128)(2,1)S(1)} copy-done((bf16[2,1,1024,1024]{3,2,1,0:T(8,128)(2,1)S(1)}, bf16[2,1,1024,1024]{3,2,1,0:T(8,128)(2,1)}, u32[]{:S(2)}) %copy-start.1) | copy-done | bytes 4194328
  23.4 0.9 pack_kv.2
  24.2 0.0 copy-start.7
  24.3 0.8 copy-done.7
  25.0 0.8 copy-done.8
  25.8 0.6 pad_add_fusion.me_ref
  26.4 14.9 %collective-permute-done.2.refs_3_ = bf16[2,1024,128]{2,1,0:T(8,128)(2,1)} collective-permute-done((bf16[2,1024,128]{2,1,0:T(8,128)(2,1)S(1)}, bf16[2,1024,128]{2,1,0:T(8,128)(2,1)}, u32[]{:S(2)}, u32[]{:S(2)}) %collective-permute-start.2) | collective-permute-done | bytes 524320 | tf_op jit(solution)/shard_map/ppermute | solution.py:522
  41.4 0.0 collective-permute-done.3.refs_4_
  41.4 1.2 collective-permute-start.4
  42.6 1.2 collective-permute-start.5
  43.7 3.9 %collective-permute-start.6 = (bf16[2,1024,128]{2,1,0:T(8,128)(2,1)S(1)}, bf16[2,1024,128]{2,1,0:T(8,128)(2,1)}, u32[]{:S(2)}, u32[]{:S(2)}) collective-permute-start(bf16[2,1024,128]{2,1,0:T(8,128)(2,1)S(1)} %get-tuple-element.50), channel_id=1, source_target_pairs={{0,13},{1,14},{2,15},{3,12},{4,1},{5,2},{6,3},{7,0},{8,5},{9,6},{1... | collective-permute-start | bytes 1572872 | tf_op jit(solution)/shard_map/ppermute | solution.py:522
  47.6 0.0 collective-permute-done.refs_1_
  47.6 0.0 collective-permute-done.1.refs_2_
  47.6 0.0 all-to-all-done.q_in
  47.6 15.1 %attend_near.1 = (f32[64,80,128]{2,1,0:T(8,128)}, f32[64,80,128]{2,1,0:T(8,128)}) custom-call(s32[2]{0:T(128)} %pad_add_fusion.me_ref, s32[16]{0:T(128)} %lengths.5, bf16[16,336,128]{2,1,0:T(8,128)(2,1)} %all-to-all-done.q_in, bf16[2,1024,128]{2,1,0:T(8,128)(2,1)} %copy-done.7, bf16[2,1024,128]{2,1,0:T(8,128)(2,1)} %collective-permute-done.refs_1_, ...), custom_call_target="tpu_custom_call" | custom-call | flops 10000000000 | bytes 10000000 | tf_op jit(solution)/shard_map/attend_near/pallas_call | solution.py:297
  62.7 1.0 collective-permute-done.4.refs_5_.refs_0_
  63.7 0.0 collective-permute-done.5.refs_6_.refs_1_
  63.7 0.0 collective-permute-done.6.refs_7_.refs_2_
  63.7 0.8 copy-done.10
  64.5 4.4 %all-to-all-start.1 = ((bf16[16,336,128]{2,1,0:T(8,128)(2,1)}), bf16[16,336,128]{2,1,0:T(8,128)(2,1)S(1)}, u32[]{:S(2)}, u32[]{:S(2)}) async-start(bf16[16,336,128]{2,1,0:T(8,128)(2,1)} %get-tuple-element.54), calls=%async_computation.1 | async-start | bytes 2752512 | tf_op jit(solution)/shard_map/all_to_all | solution.py:525
  68.9 11.7 %attend.3 = bf16[16,336,128]{2,1,0:T(8,128)(2,1)} custom-call(s32[2]{0:T(128)} %pad_add_fusion.me_ref, s32[16]{0:T(128)} %lengths.5, bf16[16,336,128]{2,1,0:T(8,128)(2,1)} %all-to-all-done.q_in, bf16[2,1024,128]{2,1,0:T(8,128)(2,1)} %copy-done.10, bf16[2,1024,128]{2,1,0:T(8,128)(2,1)} %collective-permute-done.5.refs_6_.refs_1_, ...), custom_call_target="tpu_custom_call" | custom-call | flops 6000000000 | bytes 6000000 | tf_op jit(solution)/shard_map/attend/pallas_call | solution.py:297
  80.6 13.6 %all-to-all-done.1.q_in = bf16[16,336,128]{2,1,0:T(8,128)(2,1)S(1)} async-done(((bf16[16,336,128]{2,1,0:T(8,128)(2,1)}), bf16[16,336,128]{2,1,0:T(8,128)(2,1)S(1)}, u32[]{:S(2)}, u32[]{:S(2)}) %all-to-all-start.1) | async-done | bytes 1376288 | tf_op jit(solution)/shard_map/all_to_all | solution.py:525
  94.2 1.1 copy-done.9
  95.3 3.7 %all-to-all-start.3 = ((bf16[16,336,128]{2,1,0:T(8,128)(2,1)}), bf16[16,336,128]{2,1,0:T(8,128)(2,1)S(1)}, u32[]{:S(2)}, u32[]{:S(2)}) async-start(bf16[16,336,128]{2,1,0:T(8,128)(2,1)} %attend.3), calls=%async_computation.3 | async-start | bytes 2752512 | tf_op jit(solution)/shard_map/all_to_all | solution.py:525
  99.0 18.7 %attend.2 = bf16[16,336,128]{2,1,0:T(8,128)(2,1)} custom-call(s32[2]{0:T(128)} %pad_add_fusion.me_ref, s32[16]{0:T(128)} %lengths.5, bf16[16,336,128]{2,1,0:T(8,128)(2,1)} %copy-done.9, bf16[2,1024,128]{2,1,0:T(8,128)(2,1)} %copy-done.7, bf16[2,1024,128]{2,1,0:T(8,128)(2,1)} %collective-permute-done.refs_1_, ...), custom_call_target="tpu_custom_call" | custom-call | flops 16000000000 | bytes 16000000 | tf_op jit(solution)/shard_map/attend/pallas_call | solution.py:297
  117.7 0.0 copy-start.6
  117.7 4.3 %all-to-all-done.3.back_ref.codes_ref = bf16[16,336,128]{2,1,0:T(8,128)(2,1)S(1)} async-done(((bf16[16,336,128]{2,1,0:T(8,128)(2,1)}), bf16[16,336,128]{2,1,0:T(8,128)(2,1)S(1)}, u32[]{:S(2)}, u32[]{:S(2)}) %all-to-all-start.3) | async-done | bytes 1376288 | tf_op jit(solution)/shard_map/all_to_all | solution.py:525
  122.0 8.8 %all-to-all-start.2 = ((bf16[16,336,128]{2,1,0:T(8,128)(2,1)}), bf16[16,336,128]{2,1,0:T(8,128)(2,1)S(1)}, u32[]{:S(2)}, u32[]{:S(2)}) async-start(bf16[16,336,128]{2,1,0:T(8,128)(2,1)} %attend.2), calls=%async_computation.2 | async-start | bytes 2752512 | tf_op jit(solution)/shard_map/all_to_all | solution.py:525
  130.9 0.0 copy-done.6
  130.9 0.0 copy-start.3
  130.9 1.3 copy-done.3
  132.2 1.9 %attend_self.1 = (f32[8,320,128]{2,1,0:T(8,128)S(1)}, f32[8,320,128]{2,1,0:T(8,128)S(1)}, f32[8,8,128]{2,1,0:T(8,128)S(1)}) custom-call(bf16[128,5120]{1,0:T(8,128)(2,1)S(1)} %copy-done.3, bf16[2,128,1024]{2,1,0:T(8,128)(2,1)S(1)} %copy-done.6), custom_call_target="tpu_custom_call" | custom-call | tf_op jit(solution)/shard_map/attend_self/pallas_call | solution.py:442
  134.1 1.1 copy-done.4
  135.1 2.9 %merge.2.refs_0_ = f32[128,5120]{1,0:T(8,128)} custom-call(bf16[16,336,128]{2,1,0:T(8,128)(2,1)S(1)} %all-to-all-done.3.back_ref.codes_ref, bf16[16,336,128]{2,1,0:T(8,128)(2,1)S(1)} %all-to-all-done.3.back_ref.codes_ref, f32[8,320,128]{2,1,0:T(8,128)S(1)} %get-tuple-element.62.own_ref, f32[8,8,128]{2,1,0:T(8,128)S(1)} %get-tuple-element.59.own_lse), custom_call_target="tpu_custom_call" | custom-call | tf_op jit(solution)/shard_map/merge/pallas_call | solution.py:497
  138.0 12.6 %all-to-all-done.2.back_ref.codes_ref = bf16[16,336,128]{2,1,0:T(8,128)(2,1)S(1)} async-done(((bf16[16,336,128]{2,1,0:T(8,128)(2,1)}), bf16[16,336,128]{2,1,0:T(8,128)(2,1)S(1)}, u32[]{:S(2)}, u32[]{:S(2)}) %all-to-all-start.2) | async-done | bytes 1376288 | tf_op jit(solution)/shard_map/all_to_all | solution.py:525
  150.6 1.3 copy-done.5
  152.0 2.9 %merge.3 = f32[128,5120]{1,0:T(8,128)} custom-call(bf16[16,336,128]{2,1,0:T(8,128)(2,1)S(1)} %all-to-all-done.2.back_ref.codes_ref, bf16[16,336,128]{2,1,0:T(8,128)(2,1)S(1)} %all-to-all-done.2.back_ref.codes_ref, f32[8,320,128]{2,1,0:T(8,128)S(1)} %copy-done.5, f32[8,8,128]{2,1,0:T(8,128)S(1)} %get-tuple-element.59.own_lse, ...), custom_call_target="tpu_custom_call", output_to_operand_aliasing={{}: (4, {})} | custom-call | tf_op jit(solution)/shard_map/merge/pallas_call | solution.py:497
  (7 shorter events, 0.0 us)
Async XLA Ops:
  0.8 1.3 copy-start.2
  4.5 43.1 %all-to-all-start = ((bf16[16,336,128]{2,1,0:T(8,128)(2,1)}), bf16[16,336,128]{2,1,0:T(8,128)(2,1)}, u32[]{:S(2)}, u32[]{:S(2)}) async-start(bf16[16,336,128]{2,1,0:T(8,128)(2,1)} %get-tuple-element.35), calls=%async_computation | async-start | bytes 2752512 | tf_op jit(solution)/shard_map/all_to_all | solution.py:525
  11.6 2.2 %copy-start = (bf16[2,1,1024,1024]{3,2,1,0:T(8,128)(2,1)S(1)}, bf16[2,1,1024,1024]{3,2,1,0:T(8,128)(2,1)}, u32[]{:S(2)}) copy-start(bf16[2,1,1024,1024]{3,2,1,0:T(8,128)(2,1)} %kv_ref.4) | copy-start | bytes 12582916
  14.6 26.7 %collective-permute-start.2 = (bf16[2,1024,128]{2,1,0:T(8,128)(2,1)S(1)}, bf16[2,1024,128]{2,1,0:T(8,128)(2,1)}, u32[]{:S(2)}, u32[]{:S(2)}) collective-permute-start(bf16[2,1024,128]{2,1,0:T(8,128)(2,1)S(1)} %get-tuple-element.39), channel_id=1, source_target_pairs={{0,4},{1,5},{2,6},{3,7},{4,8},{5,9},{6,10},{7,11},{8,12},{9,13},{1... | collective-permute-start | bytes 1572872 | tf_op jit(solution)/shard_map/ppermute | solution.py:522
  16.6 24.8 %collective-permute-start.3 = (bf16[2,1024,128]{2,1,0:T(8,128)(2,1)S(1)}, bf16[2,1024,128]{2,1,0:T(8,128)(2,1)}, u32[]{:S(2)}, u32[]{:S(2)}) collective-permute-start(bf16[2,1024,128]{2,1,0:T(8,128)(2,1)S(1)} %get-tuple-element.40), channel_id=1, source_target_pairs={{0,12},{1,13},{2,14},{3,15},{4,0},{5,1},{6,2},{7,3},{8,4},{9,5},{1... | collective-permute-start | bytes 1572872 | tf_op jit(solution)/shard_map/ppermute | solution.py:522
  17.9 29.7 %collective-permute-start = (bf16[2,1024,128]{2,1,0:T(8,128)(2,1)S(1)}, bf16[2,1024,128]{2,1,0:T(8,128)(2,1)}, u32[]{:S(2)}, u32[]{:S(2)}) collective-permute-start(bf16[2,1024,128]{2,1,0:T(8,128)(2,1)S(1)} %get-tuple-element.37), channel_id=1, source_target_pairs={{0,1},{1,2},{2,3},{3,0},{4,5},{5,6},{6,7},{7,4},{8,9},{9,10},{10,1... | collective-permute-start | bytes 1572872 | tf_op jit(solution)/shard_map/ppermute | solution.py:522
  19.8 27.8 %collective-permute-start.1 = (bf16[2,1024,128]{2,1,0:T(8,128)(2,1)S(1)}, bf16[2,1024,128]{2,1,0:T(8,128)(2,1)}, u32[]{:S(2)}, u32[]{:S(2)}) collective-permute-start(bf16[2,1024,128]{2,1,0:T(8,128)(2,1)S(1)} %get-tuple-element.38), channel_id=1, source_target_pairs={{0,3},{1,0},{2,1},{3,2},{4,7},{5,4},{6,5},{7,6},{8,11},{9,8},{10,9... | collective-permute-start | bytes 1572872 | tf_op jit(solution)/shard_map/ppermute | solution.py:522
  21.2 2.2 %copy-start.1 = (bf16[2,1,1024,1024]{3,2,1,0:T(8,128)(2,1)S(1)}, bf16[2,1,1024,1024]{3,2,1,0:T(8,128)(2,1)}, u32[]{:S(2)}) copy-start(bf16[2,1,1024,1024]{3,2,1,0:T(8,128)(2,1)} %kv_ref.4) | copy-start | bytes 12582916
  24.2 0.8 copy-start.7
  25.0 0.8 copy-start.8
  41.4 22.3 %collective-permute-start.4 = (bf16[2,1024,128]{2,1,0:T(8,128)(2,1)}, bf16[2,1024,128]{2,1,0:T(8,128)(2,1)S(1)}, u32[]{:S(2)}, u32[]{:S(2)}) collective-permute-start(bf16[2,1024,128]{2,1,0:T(8,128)(2,1)} %copy-done.8), channel_id=1, source_target_pairs={{0,8},{1,9},{2,10},{3,11},{4,12},{5,13},{6,14},{7,15},{8,0},{9,1},... | collective-permute-start | bytes 1572872 | tf_op jit(solution)/shard_map/ppermute | solution.py:522
  42.6 21.1 %collective-permute-start.5 = (bf16[2,1024,128]{2,1,0:T(8,128)(2,1)S(1)}, bf16[2,1024,128]{2,1,0:T(8,128)(2,1)}, u32[]{:S(2)}, u32[]{:S(2)}) collective-permute-start(bf16[2,1024,128]{2,1,0:T(8,128)(2,1)S(1)} %get-tuple-element.49), channel_id=1, source_target_pairs={{0,5},{1,6},{2,7},{3,4},{4,9},{5,10},{6,11},{7,8},{8,13},{9,14},{1... | collective-permute-start | bytes 1572872 | tf_op jit(solution)/shard_map/ppermute | solution.py:522
  43.7 20.0 %collective-permute-start.6 = (bf16[2,1024,128]{2,1,0:T(8,128)(2,1)S(1)}, bf16[2,1024,128]{2,1,0:T(8,128)(2,1)}, u32[]{:S(2)}, u32[]{:S(2)}) collective-permute-start(bf16[2,1024,128]{2,1,0:T(8,128)(2,1)S(1)} %get-tuple-element.50), channel_id=1, source_target_pairs={{0,13},{1,14},{2,15},{3,12},{4,1},{5,2},{6,3},{7,0},{8,5},{9,6},{1... | collective-permute-start | bytes 1572872 | tf_op jit(solution)/shard_map/ppermute | solution.py:522
  63.7 0.8 copy-start.10
  64.5 29.7 %all-to-all-start.1 = ((bf16[16,336,128]{2,1,0:T(8,128)(2,1)}), bf16[16,336,128]{2,1,0:T(8,128)(2,1)S(1)}, u32[]{:S(2)}, u32[]{:S(2)}) async-start(bf16[16,336,128]{2,1,0:T(8,128)(2,1)} %get-tuple-element.54), calls=%async_computation.1 | async-start | bytes 2752512 | tf_op jit(solution)/shard_map/all_to_all | solution.py:525
  94.2 1.1 copy-start.9
  95.3 26.7 %all-to-all-start.3 = ((bf16[16,336,128]{2,1,0:T(8,128)(2,1)}), bf16[16,336,128]{2,1,0:T(8,128)(2,1)S(1)}, u32[]{:S(2)}, u32[]{:S(2)}) async-start(bf16[16,336,128]{2,1,0:T(8,128)(2,1)} %attend.3), calls=%async_computation.3 | async-start | bytes 2752512 | tf_op jit(solution)/shard_map/all_to_all | solution.py:525
  117.7 13.2 %copy-start.6 = (bf16[2,128,1024]{2,1,0:T(8,128)(2,1)S(1)}, bf16[2,128,1024]{2,1,0:T(8,128)(2,1)}, u32[]{:S(2)}) copy-start(bf16[2,128,1024]{2,1,0:T(8,128)(2,1)} %kv_ref.5) | copy-start | bytes 1572868
  122.0 28.6 %all-to-all-start.2 = ((bf16[16,336,128]{2,1,0:T(8,128)(2,1)}), bf16[16,336,128]{2,1,0:T(8,128)(2,1)S(1)}, u32[]{:S(2)}, u32[]{:S(2)}) async-start(bf16[16,336,128]{2,1,0:T(8,128)(2,1)} %attend.2), calls=%async_computation.2 | async-start | bytes 2752512 | tf_op jit(solution)/shard_map/all_to_all | solution.py:525
  130.9 1.3 copy-start.3
  134.1 1.1 copy-start.4
  150.6 1.3 copy-start.5
where the time goes:
time: 153 us; the launch traced here: 155 us
  Pallas kernels  57.2 us (37%)
  waiting for transfers between devices  46.5 us (30%)
  starting transfers between devices  36.8 us (24%)
  local copies, waits for them, and re-layouts  13.6 us (9%)
    pallas_call x3, Pallas kernels, attend(): pl.pallas_call(functools.partial(attend_kernel, slots, C, U, first, last)...  45.4 us
    all_to_all x4, waiting for transfers between devices, swap(): return lax.all_to_all(x, 'node', split_axis=0, concat_axis=0, tiled=True)  30.6 us
    all_to_all x4, starting transfers between devices, swap(): return lax.all_to_all(x, 'node', split_axis=0, concat_axis=0, tiled=True)  24 us
    ppermute x7, waiting for transfers between devices, travel(): return lax.ppermute(piece, ('leaf', 'node'), travel_pairs(i))  15.9 us
    unnamed x23, local copies, waits for them, and re-layouts  13.6 us
    ppermute x7, starting transfers between devices, travel(): return lax.ppermute(piece, ('leaf', 'node'), travel_pairs(i))  12.7 us
    pallas_call x2, Pallas kernels, merge(): pl.pallas_call(functools.partial(merge_kernel, part), grid=(LV,), out_sha...  5.79 us
  transfers between devices with their start and end apart: 11, of which 5 were waited for; matrix products, arithmetic and copies ran while one was open for 0% of the time, Pallas kernels for 34%

commit v1 on v0

--- a/solution.py
+++ b/solution.py
@@ -300,7 +300,7 @@
         in_specs=[smem] * 2 + [hbm] * (1 + held + len(extra)),
         out_specs=out_specs,
         scratch_shapes=scratch,
-        compiler_params=pltpu.CompilerParams(vmem_limit_bytes=62 * 1024 * 1024),
+        compiler_params=pltpu.CompilerParams(vmem_limit_bytes=(60 if first and last else 62) * 1024 * 1024),
         cost_estimate=pl.CostEstimate(
             flops=held * 2_000_000_000, bytes_accessed=held * 2_000_000, transcendentals=held * 1_000_000
         ),

time: 153 us -> 153 us (level)
  the two profiles are of different devices: /device:TPU:96 before, /device:TPU:1 now
where the time goes in v1:
time: 153 us; the launch traced here: 152 us
  Pallas kernels  62.3 us (41%)
  waiting for transfers between devices  40.2 us (26%)
  starting transfers between devices  36.2 us (24%)
  local copies, waits for them, and re-layouts  12.8 us (8%)
    pallas_call x3, Pallas kernels, attend(): pl.pallas_call(functools.partial(attend_kernel, slots, C, U, first, last)...  50.5 us
    all_to_all x4, starting transfers between devices, swap(): return lax.all_to_all(x, 'node', split_axis=0, concat_axis=0, tiled=True)  26.6 us
    all_to_all x4, waiting for transfers between devices, swap(): return lax.all_to_all(x, 'node', split_axis=0, concat_axis=0, tiled=True)  20.3 us
    ppermute x7, waiting for transfers between devices, travel(): return lax.ppermute(piece, ('leaf', 'node'), travel_pairs(i))  19.9 us
    unnamed x23, local copies, waits for them, and re-layouts  12.8 us
    ppermute x7, starting transfers between devices, travel(): return lax.ppermute(piece, ('leaf', 'node'), travel_pairs(i))  9.57 us
    pallas_call x2, Pallas kernels, merge(): pl.pallas_call(functools.partial(merge_kernel, part), grid=(LV,), out_sha...  5.79 us
  transfers between devices with their start and end apart: 11, of which 4 were waited for; matrix products, arithmetic and copies ran while one was open for 0% of the time, Pallas kernels for 37%

profile of v1, /device:TPU:1, one launch (start us, length us, event | category | flops | bytes accessed | tf_op | source)
XLA Modules:
  0.0 152.3 jit_solution(5998227541299583975)
XLA Ops:
  0.0 0.8 copy.7.anc
  0.8 1.3 copy-done.2
  2.1 2.4 %pack_queries.1 = (bf16[16,336,128]{2,1,0:T(8,128)(2,1)}, bf16[16,336,128]{2,1,0:T(8,128)(2,1)}) custom-call(s32[8,3]{1,0:T(8,128)S(1)} %copy.7.anc, bf16[128,5120]{1,0:T(8,128)(2,1)S(1)} %copy-done.2), custom_call_target="tpu_custom_call" | custom-call | tf_op jit(solution)/shard_map/pack_queries/pallas_call | solution.py:354
  4.5 7.6 %all-to-all-start = ((bf16[16,336,128]{2,1,0:T(8,128)(2,1)}), bf16[16,336,128]{2,1,0:T(8,128)(2,1)}, u32[]{:S(2)}, u32[]{:S(2)}) async-start(bf16[16,336,128]{2,1,0:T(8,128)(2,1)} %get-tuple-element.35), calls=%async_computation | async-start | bytes 2752512 | tf_op jit(solution)/shard_map/all_to_all | solution.py:525
  12.1 0.0 copy-start
  12.1 2.2 %copy-done = bf16[2,1,1024,1024]{3,2,1,0:T(8,128)(2,1)S(1)} copy-done((bf16[2,1,1024,1024]{3,2,1,0:T(8,128)(2,1)S(1)}, bf16[2,1,1024,1024]{3,2,1,0:T(8,128)(2,1)}, u32[]{:S(2)}) %copy-start) | copy-done | bytes 4194328
  14.3 0.9 pack_kv.3
  15.2 1.4 collective-permute-start.2
  16.6 1.4 collective-permute-start.3
  17.9 1.3 collective-permute-start
  19.3 1.4 collective-permute-start.1
  20.6 2.2 %copy-done.1 = bf16[2,1,1024,1024]{3,2,1,0:T(8,128)(2,1)S(1)} copy-done((bf16[2,1,1024,1024]{3,2,1,0:T(8,128)(2,1)S(1)}, bf16[2,1,1024,1024]{3,2,1,0:T(8,128)(2,1)}, u32[]{:S(2)}) %copy-start.1) | copy-done | bytes 4194328
  22.8 0.9 pack_kv.2
  23.7 0.0 copy-start.7
  23.7 0.8 copy-done.7
  24.5 0.8 copy-done.8
  25.3 0.6 pad_add_fusion.me_ref
  25.9 16.1 %collective-permute-done.2.refs_3_ = bf16[2,1024,128]{2,1,0:T(8,128)(2,1)} collective-permute-done((bf16[2,1024,128]{2,1,0:T(8,128)(2,1)S(1)}, bf16[2,1024,128]{2,1,0:T(8,128)(2,1)}, u32[]{:S(2)}, u32[]{:S(2)}) %collective-permute-start.2) | collective-permute-done | bytes 524320 | tf_op jit(solution)/shard_map/ppermute | solution.py:522
  42.0 0.0 collective-permute-done.3.refs_4_
  42.0 2.4 %collective-permute-start.4 = (bf16[2,1024,128]{2,1,0:T(8,128)(2,1)}, bf16[2,1024,128]{2,1,0:T(8,128)(2,1)S(1)}, u32[]{:S(2)}, u32[]{:S(2)}) collective-permute-start(bf16[2,1024,128]{2,1,0:T(8,128)(2,1)} %copy-done.8), channel_id=1, source_target_pairs={{0,8},{1,9},{2,10},{3,11},{4,12},{5,13},{6,14},{7,15},{8,0},{9,1},... | collective-permute-start | bytes 1572872 | tf_op jit(solution)/shard_map/ppermute | solution.py:522
  44.4 1.0 collective-permute-start.5
  45.4 0.7 collective-permute-start.6
  46.2 0.0 collective-permute-done.refs_1_
  46.2 0.0 collective-permute-done.1.refs_2_
  46.2 0.0 all-to-all-done.q_in
  46.2 14.2 %attend_near.1 = (f32[64,80,128]{2,1,0:T(8,128)}, f32[64,80,128]{2,1,0:T(8,128)}) custom-call(s32[2]{0:T(128)} %pad_add_fusion.me_ref, s32[16]{0:T(128)} %lengths.5, bf16[16,336,128]{2,1,0:T(8,128)(2,1)} %all-to-all-done.q_in, bf16[2,1024,128]{2,1,0:T(8,128)(2,1)} %copy-done.7, bf16[2,1024,128]{2,1,0:T(8,128)(2,1)} %collective-permute-done.refs_1_, ...), custom_call_target="tpu_custom_call" | custom-call | flops 10000000000 | bytes 10000000 | tf_op jit(solution)/shard_map/attend_near/pallas_call | solution.py:297
  60.4 0.0 collective-permute-done.4.refs_5_.refs_0_
  60.4 0.0 copy-start.10
  60.4 0.0 collective-permute-done.5.refs_6_.refs_1_
  60.5 3.7 %collective-permute-done.6.refs_7_.refs_2_ = bf16[2,1024,128]{2,1,0:T(8,128)(2,1)} collective-permute-done((bf16[2,1024,128]{2,1,0:T(8,128)(2,1)S(1)}, bf16[2,1024,128]{2,1,0:T(8,128)(2,1)}, u32[]{:S(2)}, u32[]{:S(2)}) %collective-permute-start.6) | collective-permute-done | bytes 524320 | tf_op jit(solution)/shard_map/ppermute | solution.py:522
  64.1 0.0 copy-done.10
  64.1 7.5 %all-to-all-start.1 = ((bf16[16,336,128]{2,1,0:T(8,128)(2,1)}), bf16[16,336,128]{2,1,0:T(8,128)(2,1)S(1)}, u32[]{:S(2)}, u32[]{:S(2)}) async-start(bf16[16,336,128]{2,1,0:T(8,128)(2,1)} %get-tuple-element.54), calls=%async_computation.1 | async-start | bytes 2752512 | tf_op jit(solution)/shard_map/all_to_all | solution.py:525
  71.7 14.5 %attend.3 = bf16[16,336,128]{2,1,0:T(8,128)(2,1)} custom-call(s32[2]{0:T(128)} %pad_add_fusion.me_ref, s32[16]{0:T(128)} %lengths.5, bf16[16,336,128]{2,1,0:T(8,128)(2,1)} %all-to-all-done.q_in, bf16[2,1024,128]{2,1,0:T(8,128)(2,1)} %copy-done.10, bf16[2,1024,128]{2,1,0:T(8,128)(2,1)} %collective-permute-done.5.refs_6_.refs_1_, ...), custom_call_target="tpu_custom_call" | custom-call | flops 6000000000 | bytes 6000000 | tf_op jit(solution)/shard_map/attend/pallas_call | solution.py:297
  86.2 8.7 %all-to-all-done.1.q_in = bf16[16,336,128]{2,1,0:T(8,128)(2,1)S(1)} async-done(((bf16[16,336,128]{2,1,0:T(8,128)(2,1)}), bf16[16,336,128]{2,1,0:T(8,128)(2,1)S(1)}, u32[]{:S(2)}, u32[]{:S(2)}) %all-to-all-start.1) | async-done | bytes 1376288 | tf_op jit(solution)/shard_map/all_to_all | solution.py:525
  94.8 1.1 copy-done.9
  95.9 3.7 %all-to-all-start.3 = ((bf16[16,336,128]{2,1,0:T(8,128)(2,1)}), bf16[16,336,128]{2,1,0:T(8,128)(2,1)S(1)}, u32[]{:S(2)}, u32[]{:S(2)}) async-start(bf16[16,336,128]{2,1,0:T(8,128)(2,1)} %attend.3), calls=%async_computation.3 | async-start | bytes 2752512 | tf_op jit(solution)/shard_map/all_to_all | solution.py:525
  99.6 21.8 %attend.2 = bf16[16,336,128]{2,1,0:T(8,128)(2,1)} custom-call(s32[2]{0:T(128)} %pad_add_fusion.me_ref, s32[16]{0:T(128)} %lengths.5, bf16[16,336,128]{2,1,0:T(8,128)(2,1)} %copy-done.9, bf16[2,1024,128]{2,1,0:T(8,128)(2,1)} %copy-done.7, bf16[2,1024,128]{2,1,0:T(8,128)(2,1)} %collective-permute-done.refs_1_, ...), custom_call_target="tpu_custom_call" | custom-call | flops 16000000000 | bytes 16000000 | tf_op jit(solution)/shard_map/attend/pallas_call | solution.py:297
  121.5 0.0 copy-start.6
  121.5 0.0 all-to-all-done.3.back_ref.codes_ref
  121.5 7.7 %all-to-all-start.2 = ((bf16[16,336,128]{2,1,0:T(8,128)(2,1)}), bf16[16,336,128]{2,1,0:T(8,128)(2,1)S(1)}, u32[]{:S(2)}, u32[]{:S(2)}) async-start(bf16[16,336,128]{2,1,0:T(8,128)(2,1)} %attend.2), calls=%async_computation.2 | async-start | bytes 2752512 | tf_op jit(solution)/shard_map/all_to_all | solution.py:525
  129.3 0.0 copy-start.3
  129.3 1.3 copy-done.3
  130.6 1.9 %attend_self.1 = (f32[8,320,128]{2,1,0:T(8,128)S(1)}, f32[8,320,128]{2,1,0:T(8,128)S(1)}, f32[8,8,128]{2,1,0:T(8,128)S(1)}) custom-call(bf16[128,5120]{1,0:T(8,128)(2,1)S(1)} %copy-done.3, bf16[2,128,1024]{2,1,0:T(8,128)(2,1)S(1)} %copy-done.6), custom_call_target="tpu_custom_call" | custom-call | tf_op jit(solution)/shard_map/attend_self/pallas_call | solution.py:442
  132.5 1.1 copy-done.4
  133.5 2.9 %merge.2.refs_0_ = f32[128,5120]{1,0:T(8,128)} custom-call(bf16[16,336,128]{2,1,0:T(8,128)(2,1)S(1)} %all-to-all-done.3.back_ref.codes_ref, bf16[16,336,128]{2,1,0:T(8,128)(2,1)S(1)} %all-to-all-done.3.back_ref.codes_ref, f32[8,320,128]{2,1,0:T(8,128)S(1)} %get-tuple-element.62.own_ref, f32[8,8,128]{2,1,0:T(8,128)S(1)} %get-tuple-element.59.own_lse), custom_call_target="tpu_custom_call" | custom-call | tf_op jit(solution)/shard_map/merge/pallas_call | solution.py:497
  136.4 11.6 %all-to-all-done.2.back_ref.codes_ref = bf16[16,336,128]{2,1,0:T(8,128)(2,1)S(1)} async-done(((bf16[16,336,128]{2,1,0:T(8,128)(2,1)}), bf16[16,336,128]{2,1,0:T(8,128)(2,1)S(1)}, u32[]{:S(2)}, u32[]{:S(2)}) %all-to-all-start.2) | async-done | bytes 1376288 | tf_op jit(solution)/shard_map/all_to_all | solution.py:525
  148.1 1.3 copy-done.5
  149.4 2.9 %merge.3 = f32[128,5120]{1,0:T(8,128)} custom-call(bf16[16,336,128]{2,1,0:T(8,128)(2,1)S(1)} %all-to-all-done.2.back_ref.codes_ref, bf16[16,336,128]{2,1,0:T(8,128)(2,1)S(1)} %all-to-all-done.2.back_ref.codes_ref, f32[8,320,128]{2,1,0:T(8,128)S(1)} %copy-done.5, f32[8,8,128]{2,1,0:T(8,128)S(1)} %get-tuple-element.59.own_lse, ...), custom_call_target="tpu_custom_call", output_to_operand_aliasing={{}: (4, {})} | custom-call | tf_op jit(solution)/shard_map/merge/pallas_call | solution.py:497
  (7 shorter events, 0.0 us)
Async XLA Ops:
  0.8 1.3 copy-start.2
  4.5 41.7 %all-to-all-start = ((bf16[16,336,128]{2,1,0:T(8,128)(2,1)}), bf16[16,336,128]{2,1,0:T(8,128)(2,1)}, u32[]{:S(2)}, u32[]{:S(2)}) async-start(bf16[16,336,128]{2,1,0:T(8,128)(2,1)} %get-tuple-element.35), calls=%async_computation | async-start | bytes 2752512 | tf_op jit(solution)/shard_map/all_to_all | solution.py:525
  12.1 2.2 %copy-start = (bf16[2,1,1024,1024]{3,2,1,0:T(8,128)(2,1)S(1)}, bf16[2,1,1024,1024]{3,2,1,0:T(8,128)(2,1)}, u32[]{:S(2)}) copy-start(bf16[2,1,1024,1024]{3,2,1,0:T(8,128)(2,1)} %kv_ref.4) | copy-start | bytes 12582916
  15.2 26.8 %collective-permute-start.2 = (bf16[2,1024,128]{2,1,0:T(8,128)(2,1)S(1)}, bf16[2,1024,128]{2,1,0:T(8,128)(2,1)}, u32[]{:S(2)}, u32[]{:S(2)}) collective-permute-start(bf16[2,1024,128]{2,1,0:T(8,128)(2,1)S(1)} %get-tuple-element.39), channel_id=1, source_target_pairs={{0,4},{1,5},{2,6},{3,7},{4,8},{5,9},{6,10},{7,11},{8,12},{9,13},{1... | collective-permute-start | bytes 1572872 | tf_op jit(solution)/shard_map/ppermute | solution.py:522
  16.6 25.4 %collective-permute-start.3 = (bf16[2,1024,128]{2,1,0:T(8,128)(2,1)S(1)}, bf16[2,1024,128]{2,1,0:T(8,128)(2,1)}, u32[]{:S(2)}, u32[]{:S(2)}) collective-permute-start(bf16[2,1024,128]{2,1,0:T(8,128)(2,1)S(1)} %get-tuple-element.40), channel_id=1, source_target_pairs={{0,12},{1,13},{2,14},{3,15},{4,0},{5,1},{6,2},{7,3},{8,4},{9,5},{1... | collective-permute-start | bytes 1572872 | tf_op jit(solution)/shard_map/ppermute | solution.py:522
  17.9 28.2 %collective-permute-start = (bf16[2,1024,128]{2,1,0:T(8,128)(2,1)S(1)}, bf16[2,1024,128]{2,1,0:T(8,128)(2,1)}, u32[]{:S(2)}, u32[]{:S(2)}) collective-permute-start(bf16[2,1024,128]{2,1,0:T(8,128)(2,1)S(1)} %get-tuple-element.37), channel_id=1, source_target_pairs={{0,1},{1,2},{2,3},{3,0},{4,5},{5,6},{6,7},{7,4},{8,9},{9,10},{10,1... | collective-permute-start | bytes 1572872 | tf_op jit(solution)/shard_map/ppermute | solution.py:522
  19.3 26.9 %collective-permute-start.1 = (bf16[2,1024,128]{2,1,0:T(8,128)(2,1)S(1)}, bf16[2,1024,128]{2,1,0:T(8,128)(2,1)}, u32[]{:S(2)}, u32[]{:S(2)}) collective-permute-start(bf16[2,1024,128]{2,1,0:T(8,128)(2,1)S(1)} %get-tuple-element.38), channel_id=1, source_target_pairs={{0,3},{1,0},{2,1},{3,2},{4,7},{5,4},{6,5},{7,6},{8,11},{9,8},{10,9... | collective-permute-start | bytes 1572872 | tf_op jit(solution)/shard_map/ppermute | solution.py:522
  20.6 2.2 %copy-start.1 = (bf16[2,1,1024,1024]{3,2,1,0:T(8,128)(2,1)S(1)}, bf16[2,1,1024,1024]{3,2,1,0:T(8,128)(2,1)}, u32[]{:S(2)}) copy-start(bf16[2,1,1024,1024]{3,2,1,0:T(8,128)(2,1)} %kv_ref.4) | copy-start | bytes 12582916
  23.7 0.8 copy-start.7
  24.5 0.8 copy-start.8
  42.0 18.4 %collective-permute-start.4 = (bf16[2,1024,128]{2,1,0:T(8,128)(2,1)}, bf16[2,1024,128]{2,1,0:T(8,128)(2,1)S(1)}, u32[]{:S(2)}, u32[]{:S(2)}) collective-permute-start(bf16[2,1024,128]{2,1,0:T(8,128)(2,1)} %copy-done.8), channel_id=1, source_target_pairs={{0,8},{1,9},{2,10},{3,11},{4,12},{5,13},{6,14},{7,15},{8,0},{9,1},... | collective-permute-start | bytes 1572872 | tf_op jit(solution)/shard_map/ppermute | solution.py:522
  44.4 16.0 %collective-permute-start.5 = (bf16[2,1024,128]{2,1,0:T(8,128)(2,1)S(1)}, bf16[2,1024,128]{2,1,0:T(8,128)(2,1)}, u32[]{:S(2)}, u32[]{:S(2)}) collective-permute-start(bf16[2,1024,128]{2,1,0:T(8,128)(2,1)S(1)} %get-tuple-element.49), channel_id=1, source_target_pairs={{0,5},{1,6},{2,7},{3,4},{4,9},{5,10},{6,11},{7,8},{8,13},{9,14},{1... | collective-permute-start | bytes 1572872 | tf_op jit(solution)/shard_map/ppermute | solution.py:522
  45.4 18.7 %collective-permute-start.6 = (bf16[2,1024,128]{2,1,0:T(8,128)(2,1)S(1)}, bf16[2,1024,128]{2,1,0:T(8,128)(2,1)}, u32[]{:S(2)}, u32[]{:S(2)}) collective-permute-start(bf16[2,1024,128]{2,1,0:T(8,128)(2,1)S(1)} %get-tuple-element.50), channel_id=1, source_target_pairs={{0,13},{1,14},{2,15},{3,12},{4,1},{5,2},{6,3},{7,0},{8,5},{9,6},{1... | collective-permute-start | bytes 1572872 | tf_op jit(solution)/shard_map/ppermute | solution.py:522
  60.4 3.7 %copy-start.10 = (bf16[2,1024,128]{2,1,0:T(8,128)(2,1)}, bf16[2,1024,128]{2,1,0:T(8,128)(2,1)S(1)}, u32[]{:S(2)}) copy-start(bf16[2,1024,128]{2,1,0:T(8,128)(2,1)S(1)} %collective-permute-done.4.refs_5_.refs_0_) | copy-start | bytes 1572868
  64.1 30.7 %all-to-all-start.1 = ((bf16[16,336,128]{2,1,0:T(8,128)(2,1)}), bf16[16,336,128]{2,1,0:T(8,128)(2,1)S(1)}, u32[]{:S(2)}, u32[]{:S(2)}) async-start(bf16[16,336,128]{2,1,0:T(8,128)(2,1)} %get-tuple-element.54), calls=%async_computation.1 | async-start | bytes 2752512 | tf_op jit(solution)/shard_map/all_to_all | solution.py:525
  94.8 1.1 copy-start.9
  95.9 25.6 %all-to-all-start.3 = ((bf16[16,336,128]{2,1,0:T(8,128)(2,1)}), bf16[16,336,128]{2,1,0:T(8,128)(2,1)S(1)}, u32[]{:S(2)}, u32[]{:S(2)}) async-start(bf16[16,336,128]{2,1,0:T(8,128)(2,1)} %attend.3), calls=%async_computation.3 | async-start | bytes 2752512 | tf_op jit(solution)/shard_map/all_to_all | solution.py:525
  121.5 7.8 %copy-start.6 = (bf16[2,128,1024]{2,1,0:T(8,128)(2,1)S(1)}, bf16[2,128,1024]{2,1,0:T(8,128)(2,1)}, u32[]{:S(2)}) copy-start(bf16[2,128,1024]{2,1,0:T(8,128)(2,1)} %kv_ref.5) | copy-start | bytes 1572868
  121.5 26.6 %all-to-all-start.2 = ((bf16[16,336,128]{2,1,0:T(8,128)(2,1)}), bf16[16,336,128]{2,1,0:T(8,128)(2,1)S(1)}, u32[]{:S(2)}, u32[]{:S(2)}) async-start(bf16[16,336,128]{2,1,0:T(8,128)(2,1)} %attend.2), calls=%async_computation.2 | async-start | bytes 2752512 | tf_op jit(solution)/shard_map/all_to_all | solution.py:525
  129.3 1.3 copy-start.3
  132.5 1.1 copy-start.4
  148.1 1.3 copy-start.5
